TPU v7x, 32 devices: a whole 2x2x4 slice. The times are simulated.
32 devices in a mesh: section: 4 (over z), dp: 8 (over y, x, core).
Axes of the slice: x: 2, y: 2, z: 4, core: 2. Of those that a mesh axis runs over, the one named last changes fastest.
Arguments:
- grads: bfloat16 [4, 8, 20, 8192], P('section', 'dp'), may hold values from -6400 to 6400
- owners: int32 [4, 6], P('section'), may hold values from 0 to 7, as said below
- master: float32 [4, 8, 8, 8192], P('section', 'dp'), may hold values from -0.008 to 0.008
- moment: float32 [4, 8, 8, 8192], P('section', 'dp'), may hold values from -4 to 4
- second: float32 [4, 8, 8, 8192], P('section', 'dp'), may hold values from 0.01 to 1
- average: float32 [4, 8, 8, 8192], P('section', 'dp'), may hold values from -0.0001 to 0.0001
Outputs:
- weights: bfloat16 [4, 20, 8192], P('section')
- master_out: float32 [4, 8, 8, 8192], P('section', 'dp')
- moment_out: float32 [4, 8, 8, 8192], P('section', 'dp')
- second_out: float32 [4, 8, 8, 8192], P('section', 'dp')
- average_out: float32 [4, 8, 8, 8192], P('section', 'dp')
Inputs may be any that keep to these rules, and one draw needn't show every extreme that they name: The 6 tensors of one section have 6 different owners.
All inputs are finite; a program needn't handle non-finite values.
Results may differ from a plain program's by a relative error of at most 0.012.
Values may be sent and summed in bfloat16 or wider, within the bound.
A program may use at most 64 MiB of HBM per device.

v0:
```python
import jax
import jax.numpy as jnp
from jax import lax
from jax.sharding import PartitionSpec as P

STEP = 10


beta_one = 0.9
beta_two = 0.95
epsilon = 1e-08
learn_rate = 0.0003
decay_rate = 0.1
average_keep = 0.999
clip_level = 0.5


def spread(array, axis, root):
    mine = lax.axis_index(axis) == root
    return lax.psum(jnp.where(mine, array, jnp.zeros_like(array)), axis)


def tensor_layout(all_rows, slot_rows, layers):
    layer_rows = all_rows // layers
    kv_rows = (layer_rows - 2 - 2 * slot_rows) // 2
    counts = [slot_rows, kv_rows, kv_rows, slot_rows, 1, 1]
    layout = []
    start = 0
    for layer in range(layers):
        for position, count in enumerate(counts):
            layout.append((start, count, 1.0 if position < 4 else 0.0))
            start = start + count
    return layout


def adamw(grad, master, moment, second, average, decay, factor):
    clipped = factor * grad
    moment_new = beta_one * moment + (1.0 - beta_one) * clipped
    second_new = beta_two * second + (1.0 - beta_two) * clipped * clipped
    direction = (
        moment_new
        / (1.0 - beta_one**STEP)
        / (jnp.sqrt(second_new / (1.0 - beta_two**STEP)) + epsilon)
    )
    master_new = master - learn_rate * (direction + decay_rate * decay * master)
    average_new = average_keep * average + (1.0 - average_keep) * master_new
    return (master_new, moment_new, second_new, average_new)


def local(grads, owners, master, moment, second, average):
    all_rows = grads.shape[2]
    width = grads.shape[3]
    slot_rows = master.shape[2]
    layer_count = owners.shape[1] // 6
    layout = tensor_layout(all_rows, slot_rows, layer_count)
    owner = owners[0]
    own_index = lax.axis_index("dp")
    replicas = lax.axis_size("dp")
    numel = lax.axis_size("section") * all_rows * width
    flat = grads[0, 0].astype(jnp.float32)
    slot_ids = jnp.arange(slot_rows).reshape(slot_rows, 1)
    used = jnp.zeros((slot_rows, 1), jnp.bool_)
    decay = jnp.zeros((slot_rows, 1), jnp.float32)
    for tensor, (start, count, flag) in enumerate(layout):
        marks = jnp.logical_and(slot_ids < count, owner[tensor] == own_index)
        used = jnp.logical_or(used, marks)
        decay = jnp.where(marks, flag, decay)
    total = lax.psum(flat.astype(jnp.bfloat16), "dp").astype(jnp.float32)
    mean = total / replicas
    squares = lax.psum(jnp.sum(mean * mean), "section")
    bucket = jnp.zeros((slot_rows, width), jnp.float32)
    for tensor, (start, count, flag) in enumerate(layout):
        rows = jnp.pad(mean[start : start + count], ((0, slot_rows - count), (0, 0)))
        marks = jnp.logical_and(slot_ids < count, owner[tensor] == own_index)
        bucket = jnp.where(marks, rows, bucket)
    factor = jnp.minimum(1.0, clip_level / jnp.sqrt(squares / numel + 1e-06))
    olds = (master[0, 0], moment[0, 0], second[0, 0], average[0, 0])
    fresh = adamw(bucket, olds[0], olds[1], olds[2], olds[3], decay, factor)
    kept = tuple(
        (jnp.where(used, new_value, old_value) for new_value, old_value in zip(fresh, olds))
    )
    new_weights = kept[0].astype(jnp.bfloat16)
    pieces = []
    for tensor, (start, count, flag) in enumerate(layout):
        pieces.append(spread(new_weights[:count], "dp", owner[tensor]))
    weights = jnp.concatenate(pieces, axis=0)
    return (
        weights[None],
        kept[0][None, None],
        kept[1][None, None],
        kept[2][None, None],
        kept[3][None, None],
    )


def solution(mesh):
    in_specs = (
        P("section", "dp", None, None),
        P("section", None),
        P("section", "dp", None, None),
        P("section", "dp", None, None),
        P("section", "dp", None, None),
        P("section", "dp", None, None),
    )
    out_specs = (
        P("section", None, None),
        P("section", "dp", None, None),
        P("section", "dp", None, None),
        P("section", "dp", None, None),
        P("section", "dp", None, None),
    )
    return jax.shard_map(local, mesh=mesh, in_specs=in_specs, out_specs=out_specs, check_vma=False)
```

profile of v0, /device:TPU:0, one launch (start us, length us, event | category | flops | bytes accessed | tf_op | source)
XLA Modules:
  0.0 207.2 jit_solution(7216089227517264737)
XLA Ops:
  7.2 0.0 all-reduce.10.cloned.1.call-start
  7.2 0.7 all-reduce.10.cloned.1.call-update
  7.9 0.0 all-reduce.12.cloned.1.call-start
  7.9 0.0 copy-start.4
  8.0 0.6 copy-done.4
  8.6 0.7 fusion.19
  17.2 50.7 %all-reduce.10.cloned.1.call-done = bf16[20,8192]{1,0:T(8,128)(2,1)} async-done(((bf16[20,8192]{1,0:T(8,128)(2,1)}), bf16[20,8192]{1,0:T(8,128)(2,1)}) %all-reduce.10.cloned.1.call-update) | async-done | bytes 327696 | tf_op jit(solution)/shard_map/psum | solution.py:68
  67.9 0.0 copy-start.1
  67.9 0.0 copy-start.2
  67.9 0.0 copy-start.3
  67.9 1.9 multiply_reduce_fusion
  69.8 0.0 copy-start
  69.8 0.1 fusion.18
  69.9 12.2 %psum.57 = f32[]{:T(128)} all-reduce(f32[]{:T(128)} %get-tuple-element.20), channel_id=1, replica_groups=mesh['section'=4,'dp'=8] {'section'}, use_global_device_ids=true, to_apply=%region_2.3 | all-reduce | flops 1 | bytes 8 | tf_op jit(solution)/shard_map/psum | solution.py:70
  82.8 0.0 copy-done.1
  82.9 0.0 copy-done.2
  82.9 0.0 copy-done.3
  82.9 0.0 copy-done
  82.9 1.1 fusion.8
  84.0 0.8 broadcast_select_fusion
  84.7 0.7 broadcast_select_fusion.2
  85.5 0.0 all-reduce.12.cloned.1.call-update
  85.5 0.0 all-reduce.14.cloned.1.call-start
  85.5 0.7 broadcast_select_fusion.1
  86.2 0.0 all-reduce.14.cloned.1.call-update
  86.2 1.0 fusion.9
  87.2 48.6 %all-reduce.12.cloned.1.call-done = (bf16[1,8192]{1,0:T(2,128)(2,1)}, bf16[1,8192]{1,0:T(2,128)(2,1)}, bf16[1,8192]{1,0:T(2,128)(2,1)}, bf16[1,8192]{1,0:T(2,128)(2,1)}) async-done(((bf16[1,8192]{1,0:T(2,128)(2,1)}, bf16[1,8192]{1,0:T(2,128)(2,1)}, bf16[1,8192]{1,0:T(2,128)(2,1)}, bf16[1,8192]{1,0:T(2,128)(2,1)}), (bf16[1,8192]{1,0:T(2,128)(2,1)}, bf16[1,8192]{1,0:T(2,128)(2,1)}, bf16[1,8192]{1,0:T(2,128)(2,1)}, ...) | async-done | bytes 65552 | tf_op jit(solution)/shard_map/psum | solution.py:20
  135.8 57.0 %all-reduce.14.cloned.1.call-done = (bf16[8,8192]{1,0:T(8,128)(2,1)}, bf16[8,8192]{1,0:T(8,128)(2,1)}) async-done(((bf16[8,8192]{1,0:T(8,128)(2,1)}, bf16[8,8192]{1,0:T(8,128)(2,1)}), (bf16[8,8192]{1,0:T(8,128)(2,1)}, bf16[8,8192]{1,0:T(8,128)(2,1)})) %all-reduce.14.cloned.1.call-update) | async-done | bytes 262160 | tf_op jit(solution)/shard_map/psum | solution.py:20
  192.8 7.9 %concatenate.3 = bf16[20,8192]{1,0:T(8,128)(2,1)} concatenate(bf16[8,8192]{1,0:T(8,128)(2,1)} %get-tuple-element.9, bf16[1,8192]{1,0:T(2,128)(2,1)} %get-tuple-element.5, bf16[1,8192]{1,0:T(2,128)(2,1)} %get-tuple-element.6, bf16[8,8192]{1,0:T(8,128)(2,1)} %get-tuple-element.10, bf16[1,8192]{1,0:T(2,128)(2,1)} %get-tuple-element.7, bf16[1,8192]{1,0:T(2,128)(2,1)} %get-tuple-element.8), dimensions={0} | concatenate | bytes 655360 | tf_op jit(solution)/shard_map/concatenate | solution.py:86
  (5 shorter events, 0.0 us)
Async XLA Ops:
  7.2 60.8 %all-reduce.10.cloned.1.call-start = ((), (), s32[]{:S(2)}) async-start(), calls=%async_computation | async-start | bytes 786432 | tf_op jit(solution)/shard_map/psum | solution.py:68
  7.9 127.9 %all-reduce.12.cloned.1.call-start = ((), (), s32[]{:S(2)}) async-start(), calls=%async_computation.1 | async-start | bytes 262144 | tf_op jit(solution)/shard_map/psum | solution.py:20
  7.9 0.7 copy-start.4
  67.9 14.9 %copy-start.1 = (f32[1,1,8,8192]{3,2,1,0:T(8,128)S(1)}, f32[1,1,8,8192]{3,2,1,0:T(8,128)}, u32[]{:S(2)}) copy-start(f32[1,1,8,8192]{3,2,1,0:T(8,128)} %param.10) | copy-start | bytes 786436
  67.9 14.9 %copy-start.2 = (f32[1,1,8,8192]{3,2,1,0:T(8,128)S(1)}, f32[1,1,8,8192]{3,2,1,0:T(8,128)}, u32[]{:S(2)}) copy-start(f32[1,1,8,8192]{3,2,1,0:T(8,128)} %param.9) | copy-start | bytes 786436
  67.9 14.9 %copy-start.3 = (f32[1,1,8,8192]{3,2,1,0:T(8,128)S(1)}, f32[1,1,8,8192]{3,2,1,0:T(8,128)}, u32[]{:S(2)}) copy-start(f32[1,1,8,8192]{3,2,1,0:T(8,128)} %param.11) | copy-start | bytes 786436
  69.8 13.1 %copy-start = (f32[1,1,8,8192]{3,2,1,0:T(8,128)S(1)}, f32[1,1,8,8192]{3,2,1,0:T(8,128)}, u32[]{:S(2)}) copy-start(f32[1,1,8,8192]{3,2,1,0:T(8,128)} %param.8) | copy-start | bytes 786436
  85.5 107.3 %all-reduce.14.cloned.1.call-start = ((), (), s32[]{:S(2)}) async-start(), calls=%async_computation.2 | async-start | bytes 524288 | tf_op jit(solution)/shard_map/psum | solution.py:20
Sparse Core Ops, SparseCore 0:
  11.1 56.8 all-reduce.9
  85.6 50.1 all-reduce.11
  139.8 52.9 all-reduce.13
where the time goes:
time: 208 us; the launch traced here: 207 us
  waiting for transfers between devices  157 us (75%)
  between operations  22.4 us (11%)
  blocking collectives  12.2 us (6%)
  local copies, waits for them, and re-layouts  9.32 us (4%)
  other arithmetic  6.17 us (3%)
    psum x2, waiting for transfers between devices, spread(): return lax.psum(jnp.where(mine, array, jnp.zeros_like(array)), axis)  106 us
    psum x1, waiting for transfers between devices, local(): total = lax.psum(flat.astype(jnp.bfloat16), 'dp').astype(jnp.float32)  50.7 us
    psum x1, blocking collectives, local(): squares = lax.psum(jnp.sum(mean * mean), 'section')  12.2 us
    concatenate x1, local copies, waits for them, and re-layouts, local(): weights = jnp.concatenate(pieces, axis=0)  7.9 us
  transfers between devices with their start and end apart: 3, of which 3 were waited for; matrix products, arithmetic and copies ran while one was open for 1% of the time, Pallas kernels for 0%

commit v1 on v0

v1 whole, which is shorter than its diff:
```python
import functools

import jax
import jax.numpy as jnp
from jax import lax
from jax.experimental import pallas as pl
from jax.experimental.pallas import tpu as pltpu
from jax.sharding import PartitionSpec as P

STEP = 10


beta_one = 0.9
beta_two = 0.95
epsilon = 1e-08
learn_rate = 0.0003
decay_rate = 0.1
average_keep = 0.999
clip_level = 0.5

MESH = pl.DeviceIdType.MESH
f32 = jnp.float32
bf16 = jnp.bfloat16


def tensor_layout(all_rows, slot_rows, layers):
    layer_rows = all_rows // layers
    kv_rows = (layer_rows - 2 - 2 * slot_rows) // 2
    counts = [slot_rows, kv_rows, kv_rows, slot_rows, 1, 1]
    layout = []
    start = 0
    for layer in range(layers):
        for position, count in enumerate(counts):
            layout.append((start, count, 1.0 if position < 4 else 0.0))
            start = start + count
    return layout


def adam_master(grad, master, moment, second, decay, factor):
    clipped = factor * grad
    moment_new = beta_one * moment + (1.0 - beta_one) * clipped
    second_new = beta_two * second + (1.0 - beta_two) * clipped * clipped
    direction = (
        moment_new
        / (1.0 - beta_one**STEP)
        / (jnp.sqrt(second_new / (1.0 - beta_two**STEP)) + epsilon)
    )
    master_new = master - learn_rate * (direction + decay_rate * decay * master)
    return master_new, moment_new, second_new


def clip_factor(tile, numel):
    squares = jnp.sum(tile, keepdims=True)
    return jnp.minimum(1.0, clip_level / jnp.sqrt(squares / numel + 1e-06))


def fold(x):
    half = x.shape[1] // 2
    return jnp.concatenate([x[:, :half], x[:, half:]], axis=0).astype(bf16)


def unfold(x):
    half = x.shape[0] // 2
    return jnp.concatenate([x[:half], x[half:]], axis=1)


def exchange(
    n, ns, layout, numel,
    grads, owners, master, moment, second,
    w_out, bucket_out, sq_out,
    state, st_send, st_recv, g_recv, tot, bk_send, w_rows, q_send, q_recv, s_send, s_recv,
    local_sem, g_sems, st_sems, bk_sems, q_sems, s_sems, w_sems,
):
    me = lax.axis_index("dp")
    sec = lax.axis_index("section")
    rows, width = w_out.shape
    cw = width // n
    slot_rows = state.shape[1]
    tensors = len(layout)

    def after(d):
        return lax.rem(me + d, n)

    def before(d):
        return lax.rem(me + (n - d), n)

    def cols(index):
        return pl.ds(pl.multiple_of(index * cw, cw), cw)

    loads = [
        pltpu.make_async_copy(ref.at[0, 0], state.at[k], local_sem.at[k])
        for k, ref in enumerate((master, moment, second))
    ]
    own = pltpu.make_async_copy(grads.at[0, 0, :, cols(me)], g_recv.at[0], local_sem.at[3])
    for copy in loads:
        copy.start()
    own.start()

    barrier = pltpu.get_barrier_semaphore()
    for d in range(1, n):
        pl.semaphore_signal(barrier, inc=1, device_id={"dp": after(d)}, device_id_type=MESH)
    for e in range(1, ns):
        pl.semaphore_signal(
            barrier, inc=1, device_id={"section": lax.rem(sec + e, ns)}, device_id_type=MESH
        )
    pl.semaphore_wait(barrier, n - 1 + ns - 1)

    def remote(src, dst, sems, d, target):
        copy = pltpu.make_async_remote_copy(
            src_ref=src,
            dst_ref=dst,
            send_sem=sems.at[0, d],
            recv_sem=sems.at[1, d],
            device_id=target,
            device_id_type=MESH,
        )
        copy.start()
        return copy

    g_copies = [
        remote(grads.at[0, 0, :, cols(after(d))], g_recv.at[d], g_sems, d, {"dp": after(d)})
        for d in range(1, n)
    ]

    for copy in loads:
        copy.wait()
    st_copies = []
    for d in range(n):
        place = st_recv if d == 0 else st_send
        for k in range(3):
            place[d, 2 * slot_rows * k : 2 * slot_rows * (k + 1), :] = fold(state[k, :, cols(after(d))])
        if d:
            st_copies.append(remote(st_send.at[d], st_recv.at[d], st_sems, d, {"dp": after(d)}))

    own.wait()
    total = g_recv[0].astype(f32)
    for d, copy in zip(range(1, n), g_copies):
        copy.wait_recv()
        total = total + g_recv[d].astype(f32)
    mean = total / n
    part = jnp.zeros((slot_rows, 128), f32)
    for t, (start, count, flag) in enumerate(layout):
        piece = mean[start : start + count]
        if count < slot_rows:
            piece = jnp.concatenate([piece, jnp.zeros((slot_rows - count, cw), f32)], axis=0)
        tot[t] = piece
        for c in range(0, cw, 128):
            part = part + piece[:, c : c + 128] * piece[:, c : c + 128]
    tot[tensors] = jnp.zeros((slot_rows, cw), f32)

    q_send[...] = part
    q_copies = [
        remote(q_send, q_recv.at[d], q_sems, d, {"dp": after(d)}) for d in range(1, n)
    ]

    bk_copies = []
    for d in range(n):
        target = after(d)
        mine = jnp.int32(tensors)
        for t in range(tensors):
            mine = jnp.where(owners[0, t] == target, t, mine)
        slab = fold(tot[mine])
        if d == 0:
            bucket_out[me] = slab
        else:
            bk_send[d] = slab
            bk_copies.append(
                remote(bk_send.at[d], bucket_out.at[me], bk_sems, d, {"dp": target})
            )

    for d, copy in zip(range(1, n), q_copies):
        copy.wait_recv()
        part = part + q_recv[d]
    s_send[...] = part
    s_copies = [
        remote(s_send, s_recv.at[e], s_sems, e, {"section": lax.rem(sec + e, ns)})
        for e in range(1, ns)
    ]
    for e, copy in zip(range(1, ns), s_copies):
        copy.wait_recv()
        part = part + s_recv[e]
    sq_out[...] = part
    factor = clip_factor(part, numel)

    for copy in st_copies:
        copy.wait_recv()
    for t, (start, count, flag) in enumerate(layout):
        olds = st_recv[lax.rem(me - owners[0, t] + n, n)].astype(f32)
        old = [unfold(olds[2 * slot_rows * k : 2 * slot_rows * (k + 1)]) for k in range(3)]
        fresh, _, _ = adam_master(tot[t], old[0], old[1], old[2], flag, factor)
        w_rows[start : start + count, :] = fresh[:count]
    w_out[:, cols(me)] = w_rows[...].astype(bf16)
    w_copies = [
        remote(w_out.at[:, cols(me)], w_out.at[:, cols(me)], w_sems, d, {"dp": after(d)})
        for d in range(1, n)
    ]
    for d in range(1, n):
        there = w_out.at[:, cols(before(d))]
        pltpu.make_async_copy(there, there, w_sems.at[1, d]).wait()
        place = bucket_out.at[before(d)]
        pltpu.make_async_copy(place, place, bk_sems.at[1, d]).wait()
    for copy in g_copies + st_copies + q_copies + bk_copies + s_copies + w_copies:
        copy.wait_send()


def update(
    n, layout, numel,
    owners, master, moment, second, average, bucket, squares, w_raw,
    w_out, master_out, moment_out, second_out, average_out,
    w_sem,
):
    w_copy = pltpu.make_async_copy(w_raw, w_out.at[0], w_sem)
    w_copy.start()
    me = lax.axis_index("dp")
    slot_rows, width = master.shape[2:]
    cw = width // n
    used_rows = jnp.int32(0)
    decay = jnp.float32(0.0)
    for t, (start, count, flag) in enumerate(layout):
        mine = owners[0, t] == me
        used_rows = jnp.where(mine, count, used_rows)
        decay = jnp.where(mine, flag, decay)
    used = lax.broadcasted_iota(jnp.int32, (slot_rows, cw), 0) < used_rows
    factor = clip_factor(squares[...], numel)
    for j in range(n):
        at = (0, 0, slice(None), slice(j * cw, (j + 1) * cw))
        grad = unfold(bucket[j].astype(f32))
        fresh = adam_master(grad, master[at], moment[at], second[at], decay, factor)
        kept = [
            jnp.where(used, new, old[at]) for new, old in zip(fresh, (master, moment, second))
        ]
        master_out[at] = kept[0]
        moment_out[at] = kept[1]
        second_out[at] = kept[2]
        blended = average_keep * average[at] + (1.0 - average_keep) * kept[0]
        average_out[at] = jnp.where(used, blended, average[at])
    w_copy.wait()


def local(grads, owners, master, moment, second, average):
    rows, width = grads.shape[2:]
    slot_rows = master.shape[2]
    n = lax.axis_size("dp")
    ns = lax.axis_size("section")
    cw = width // n
    layout = tensor_layout(rows, slot_rows, owners.shape[1] // 6)
    tensors = len(layout)
    numel = ns * rows * width
    vmem = pl.BlockSpec(memory_space=pltpu.VMEM)
    smem = pl.BlockSpec(memory_space=pltpu.SMEM)
    anywhere = pl.BlockSpec(memory_space=pl.ANY)
    packed = (n, 2 * slot_rows, cw // 2)
    sems = lambda count: pltpu.SemaphoreType.DMA((2, count))
    w_raw, bucket, squares = pl.pallas_call(
        functools.partial(exchange, n, ns, layout, numel),
        out_shape=(
            jax.ShapeDtypeStruct((rows, width), bf16),
            jax.ShapeDtypeStruct(packed, bf16),
            jax.ShapeDtypeStruct((slot_rows, 128), f32),
        ),
        in_specs=[anywhere, smem, anywhere, anywhere, anywhere],
        out_specs=(vmem, vmem, vmem),
        scratch_shapes=[
            pltpu.VMEM((3, slot_rows, width), f32),
            pltpu.VMEM((n, 6 * slot_rows, cw // 2), bf16),
            pltpu.VMEM((n, 6 * slot_rows, cw // 2), bf16),
            pltpu.VMEM((n, rows, cw), bf16),
            pltpu.VMEM((tensors + 1, slot_rows, cw), f32),
            pltpu.VMEM(packed, bf16),
            pltpu.VMEM((rows, cw), f32),
            pltpu.VMEM((slot_rows, 128), f32),
            pltpu.VMEM((n, slot_rows, 128), f32),
            pltpu.VMEM((slot_rows, 128), f32),
            pltpu.VMEM((ns, slot_rows, 128), f32),
            pltpu.SemaphoreType.DMA((4,)),
            sems(n), sems(n), sems(n), sems(n), sems(ns), sems(n),
        ],
        compiler_params=pltpu.CompilerParams(
            collective_id=0, has_side_effects=True, vmem_limit_bytes=24 * 2**20
        ),
        name="exchange",
    )(grads, owners, master, moment, second)
    state = jax.ShapeDtypeStruct(master.shape, f32)
    return pl.pallas_call(
        functools.partial(update, n, layout, numel),
        out_shape=(jax.ShapeDtypeStruct((1, rows, width), bf16), state, state, state, state),
        in_specs=[smem, vmem, vmem, vmem, vmem, vmem, vmem, anywhere],
        out_specs=(anywhere, vmem, vmem, vmem, vmem),
        scratch_shapes=[pltpu.SemaphoreType.DMA],
        compiler_params=pltpu.CompilerParams(vmem_limit_bytes=24 * 2**20),
        name="update",
    )(owners, master, moment, second, average, bucket, squares, w_raw)


def solution(mesh):
    in_specs = (
        P("section", "dp", None, None),
        P("section", None),
        P("section", "dp", None, None),
        P("section", "dp", None, None),
        P("section", "dp", None, None),
        P("section", "dp", None, None),
    )
    out_specs = (
        P("section", None, None),
        P("section", "dp", None, None),
        P("section", "dp", None, None),
        P("section", "dp", None, None),
        P("section", "dp", None, None),
    )
    return jax.shard_map(local, mesh=mesh, in_specs=in_specs, out_specs=out_specs, check_vma=False)
```

time: 208 us -> 34.9 us (0.17)
  waiting for transfers between devices: 157 us -> 0 us
  Pallas kernels: 0 us -> 29.4 us
  between operations: 22.4 us -> 0.69 us
  blocking collectives: 12.2 us -> 0 us
  other arithmetic: 6.17 us -> 0 us
  local copies, waits for them, and re-layouts: 9.32 us -> 4.51 us
    psum x3 -> x0, waiting for transfers between devices: 156 us -> none  [the longest x2 106 us: spread(): return lax.psum(jnp.where(mine, array, jnp.zeros_like(array)), axis)]
    pallas_call x0 -> x2, Pallas kernels: none -> 29.4 us  [the longest x1 27.2 us: local(): pl.pallas_call(functools.partial(exchange, n, ns, layout, numel), out_sha...]
    psum x1 -> x0, blocking collectives: 12.2 us -> none  [local(): squares = lax.psum(jnp.sum(mean * mean), 'section')]
    concatenate x1 -> x0, local copies, waits for them, and re-layouts: 7.9 us -> none  [local(): weights = jnp.concatenate(pieces, axis=0)]
    unnamed x10 -> x18, local copies, waits for them, and re-layouts: 0.66 us -> 4.51 us
    select_n x3 -> x0, other arithmetic: 2.14 us -> none  [spread(): return lax.psum(jnp.where(mine, array, jnp.zeros_like(array)), axis)]
    broadcast_in_dim x2 -> x0, other arithmetic: 2.1 us -> none  [the longest x1 1.1 us: local(): kept[3][None, None]]
  transfers between devices with their start and end apart: 3 -> 0, of which waited for: 3 -> 0; matrix products, arithmetic and copies ran while one was open for 1% -> 0% of each run, Pallas kernels for 0% -> 0%
where the time goes in v1:
time: 34.9 us; the launch traced here: 34.6 us
  Pallas kernels  29.4 us (84%)
  local copies, waits for them, and re-layouts  4.51 us (13%)
  between operations  0.69 us (2%)
    pallas_call x1, Pallas kernels, local(): pl.pallas_call(functools.partial(exchange, n, ns, layout, numel), out_sha...  27.2 us
    unnamed x18, local copies, waits for them, and re-layouts  4.51 us
    pallas_call x1, Pallas kernels, local(): pl.pallas_call(functools.partial(update, n, layout, numel), out_shape=(ja...  2.26 us

profile of v1, /device:TPU:0, one launch (start us, length us, event | category | flops | bytes accessed | tf_op | source)
XLA Modules:
  0.0 34.6 jit_solution(15717576169637914902)
XLA Ops:
  0.6 0.0 copy-start
  0.6 0.9 %copy-done = f32[1,1,8,8192]{3,2,1,0:T(8,128)S(1)} copy-done((f32[1,1,8,8192]{3,2,1,0:T(8,128)S(1)}, f32[1,1,8,8192]{3,2,1,0:T(8,128)}, u32[]{:S(2)}) %copy-start) | copy-done | bytes 262168
  1.6 0.0 copy-start.2
  1.6 0.9 %copy-done.2 = f32[1,1,8,8192]{3,2,1,0:T(8,128)S(1)} copy-done((f32[1,1,8,8192]{3,2,1,0:T(8,128)S(1)}, f32[1,1,8,8192]{3,2,1,0:T(8,128)}, u32[]{:S(2)}) %copy-start.2) | copy-done | bytes 262168
  2.5 0.0 copy-start.4
  2.5 0.9 %copy-done.4 = f32[1,1,8,8192]{3,2,1,0:T(8,128)S(1)} copy-done((f32[1,1,8,8192]{3,2,1,0:T(8,128)S(1)}, f32[1,1,8,8192]{3,2,1,0:T(8,128)}, u32[]{:S(2)}) %copy-start.4) | copy-done | bytes 262168
  3.5 0.0 copy-start.6
  3.5 1.0 %copy-done.6 = bf16[1,1,20,8192]{3,2,1,0:T(8,128)(2,1)S(1)} copy-done((bf16[1,1,20,8192]{3,2,1,0:T(8,128)(2,1)S(1)}, bf16[1,1,20,8192]{3,2,1,0:T(8,128)(2,1)}, u32[]{:S(2)}) %copy-start.6) | copy-done | bytes 327704
  4.5 0.0 copy-start.8
  4.5 0.7 %copy-done.8 = s32[1,6]{1,0:T(1,128)S(1)} copy-done((s32[1,6]{1,0:T(1,128)S(1)}, s32[1,6]{1,0:T(1,128)}, u32[]{:S(2)}) %copy-start.8) | copy-done | bytes 48
  5.1 0.0 copy-start.1
  5.1 0.0 copy-start.3
  5.1 0.0 copy-start.5
  5.1 0.0 copy-start.7
  5.1 27.2 %exchange.1 = (bf16[20,8192]{1,0:T(8,128)(2,1)S(1)}, bf16[8,16,512]{2,1,0:T(8,128)(2,1)S(1)}, f32[8,128]{1,0:T(8,128)S(1)}) custom-call(bf16[1,1,20,8192]{3,2,1,0:T(8,128)(2,1)S(1)} %copy-done.6, s32[1,6]{1,0:T(1,128)S(1)} %copy-done.8, f32[1,1,8,8192]{3,2,1,0:T(8,128)S(1)} %copy-done, f32[1,1,8,8192]{3,2,1,0:T(8,128)S(1)} %copy-done.2, ...), custom_call_target="tpu_custom_call" | custom-call | tf_op jit(solution)/shard_map/exchange/pallas_call | solution.py:254
  32.3 0.0 copy-done.1
  32.3 0.0 copy-done.3
  32.4 0.0 copy-done.5
  32.4 0.0 copy-done.7
  32.4 2.3 %update.1 = (bf16[1,20,8192]{2,1,0:T(8,128)(2,1)}, f32[1,1,8,8192]{3,2,1,0:T(8,128)}, f32[1,1,8,8192]{3,2,1,0:T(8,128)}, f32[1,1,8,8192]{3,2,1,0:T(8,128)}, f32[1,1,8,8192]{3,2,1,0:T(8,128)}) custom-call(s32[1,6]{1,0:T(1,128)S(1)} %copy-done.8, f32[1,1,8,8192]{3,2,1,0:T(8,128)S(1)} %copy-done.1, f32[1,1,8,8192]{3,2,1,0:T(8,128)S(1)} %copy-done.3, ...), custom_call_target="tpu_custom_call" | custom-call | tf_op jit(solution)/shard_map/update/pallas_call | solution.py:284
Async XLA Ops:
  0.6 1.0 %copy-start = (f32[1,1,8,8192]{3,2,1,0:T(8,128)S(1)}, f32[1,1,8,8192]{3,2,1,0:T(8,128)}, u32[]{:S(2)}) copy-start(f32[1,1,8,8192]{3,2,1,0:T(8,128)} %master.3) | copy-start | bytes 786436
  1.6 0.9 %copy-start.2 = (f32[1,1,8,8192]{3,2,1,0:T(8,128)S(1)}, f32[1,1,8,8192]{3,2,1,0:T(8,128)}, u32[]{:S(2)}) copy-start(f32[1,1,8,8192]{3,2,1,0:T(8,128)} %moment.3) | copy-start | bytes 786436
  2.5 0.9 %copy-start.4 = (f32[1,1,8,8192]{3,2,1,0:T(8,128)S(1)}, f32[1,1,8,8192]{3,2,1,0:T(8,128)}, u32[]{:S(2)}) copy-start(f32[1,1,8,8192]{3,2,1,0:T(8,128)} %second.3) | copy-start | bytes 786436
  3.5 1.0 %copy-start.6 = (bf16[1,1,20,8192]{3,2,1,0:T(8,128)(2,1)S(1)}, bf16[1,1,20,8192]{3,2,1,0:T(8,128)(2,1)}, u32[]{:S(2)}) copy-start(bf16[1,1,20,8192]{3,2,1,0:T(8,128)(2,1)} %grads.1) | copy-start | bytes 983044
  4.5 0.7 %copy-start.8 = (s32[1,6]{1,0:T(1,128)S(1)}, s32[1,6]{1,0:T(1,128)}, u32[]{:S(2)}) copy-start(s32[1,6]{1,0:T(1,128)} %owners.3) | copy-start | bytes 76
  5.1 27.2 %copy-start.1 = (f32[1,1,8,8192]{3,2,1,0:T(8,128)S(1)}, f32[1,1,8,8192]{3,2,1,0:T(8,128)}, u32[]{:S(2)}) copy-start(f32[1,1,8,8192]{3,2,1,0:T(8,128)} %master.3) | copy-start | bytes 786436
  5.1 27.2 %copy-start.3 = (f32[1,1,8,8192]{3,2,1,0:T(8,128)S(1)}, f32[1,1,8,8192]{3,2,1,0:T(8,128)}, u32[]{:S(2)}) copy-start(f32[1,1,8,8192]{3,2,1,0:T(8,128)} %moment.3) | copy-start | bytes 786436
  5.1 27.2 %copy-start.5 = (f32[1,1,8,8192]{3,2,1,0:T(8,128)S(1)}, f32[1,1,8,8192]{3,2,1,0:T(8,128)}, u32[]{:S(2)}) copy-start(f32[1,1,8,8192]{3,2,1,0:T(8,128)} %second.3) | copy-start | bytes 786436
  5.1 27.2 %copy-start.7 = (f32[1,1,8,8192]{3,2,1,0:T(8,128)S(1)}, f32[1,1,8,8192]{3,2,1,0:T(8,128)}, u32[]{:S(2)}) copy-start(f32[1,1,8,8192]{3,2,1,0:T(8,128)} %average.1) | copy-start | bytes 786436

commit v2 on v1

--- a/solution.py
+++ b/solution.py
@@ -66,9 +66,9 @@
 
 def exchange(
     n, ns, layout, numel,
-    grads, owners, master, moment, second,
-    w_out, bucket_out, sq_out,
-    state, st_send, st_recv, g_recv, tot, bk_send, w_rows, q_send, q_recv, s_send, s_recv,
+    grads, owners_hbm, master, moment, second, average,
+    w_out, master_out, moment_out, second_out, average_out,
+    owners, state, st_send, st_recv, g_recv, tot, bk_send, bk_recv, w_rows, w_send, q_send, q_recv, s_send, s_recv,
     local_sem, g_sems, st_sems, bk_sems, q_sems, s_sems, w_sems,
 ):
     me = lax.axis_index("dp")
@@ -89,12 +89,14 @@
 
     loads = [
         pltpu.make_async_copy(ref.at[0, 0], state.at[k], local_sem.at[k])
-        for k, ref in enumerate((master, moment, second))
-    ]
-    own = pltpu.make_async_copy(grads.at[0, 0, :, cols(me)], g_recv.at[0], local_sem.at[3])
+        for k, ref in enumerate((master, moment, second, average))
+    ]
+    own = pltpu.make_async_copy(grads.at[0, 0, :, cols(me)], g_recv.at[0], local_sem.at[4])
+    own_owners = pltpu.make_async_copy(owners_hbm, owners, local_sem.at[5])
     for copy in loads:
         copy.start()
     own.start()
+    own_owners.start()
 
     barrier = pltpu.get_barrier_semaphore()
     for d in range(1, n):
@@ -122,15 +124,13 @@
         for d in range(1, n)
     ]
 
-    for copy in loads:
+    for copy in loads[:3]:
         copy.wait()
-    st_copies = []
     for d in range(n):
         place = st_recv if d == 0 else st_send
         for k in range(3):
             place[d, 2 * slot_rows * k : 2 * slot_rows * (k + 1), :] = fold(state[k, :, cols(after(d))])
-        if d:
-            st_copies.append(remote(st_send.at[d], st_recv.at[d], st_sems, d, {"dp": after(d)}))
+    own_owners.wait()
 
     own.wait()
     total = g_recv[0].astype(f32)
@@ -153,6 +153,10 @@
         remote(q_send, q_recv.at[d], q_sems, d, {"dp": after(d)}) for d in range(1, n)
     ]
 
+    st_copies = [
+        remote(st_send.at[d], st_recv.at[d], st_sems, d, {"dp": after(d)}) for d in range(1, n)
+    ]
+
     bk_copies = []
     for d in range(n):
         target = after(d)
@@ -161,11 +165,11 @@
             mine = jnp.where(owners[0, t] == target, t, mine)
         slab = fold(tot[mine])
         if d == 0:
-            bucket_out[me] = slab
+            bk_recv[me] = slab
         else:
             bk_send[d] = slab
             bk_copies.append(
-                remote(bk_send.at[d], bucket_out.at[me], bk_sems, d, {"dp": target})
+                remote(bk_send.at[d], bk_recv.at[me], bk_sems, d, {"dp": target})
             )
 
     for d, copy in zip(range(1, n), q_copies):
@@ -179,7 +183,6 @@
     for e, copy in zip(range(1, ns), s_copies):
         copy.wait_recv()
         part = part + s_recv[e]
-    sq_out[...] = part
     factor = clip_factor(part, numel)
 
     for copy in st_copies:
@@ -189,31 +192,16 @@
         old = [unfold(olds[2 * slot_rows * k : 2 * slot_rows * (k + 1)]) for k in range(3)]
         fresh, _, _ = adam_master(tot[t], old[0], old[1], old[2], flag, factor)
         w_rows[start : start + count, :] = fresh[:count]
-    w_out[:, cols(me)] = w_rows[...].astype(bf16)
-    w_copies = [
-        remote(w_out.at[:, cols(me)], w_out.at[:, cols(me)], w_sems, d, {"dp": after(d)})
-        for d in range(1, n)
-    ]
+    w_send[...] = w_rows[...].astype(bf16)
+    here = w_out.at[:, cols(me)]
+    w_copies = [remote(w_send, here, w_sems, d, {"dp": after(d)}) for d in range(1, n)]
+    w_own = pltpu.make_async_copy(w_send, here, local_sem.at[6])
+    w_own.start()
+
     for d in range(1, n):
-        there = w_out.at[:, cols(before(d))]
-        pltpu.make_async_copy(there, there, w_sems.at[1, d]).wait()
-        place = bucket_out.at[before(d)]
+        place = bk_recv.at[before(d)]
         pltpu.make_async_copy(place, place, bk_sems.at[1, d]).wait()
-    for copy in g_copies + st_copies + q_copies + bk_copies + s_copies + w_copies:
-        copy.wait_send()
-
-
-def update(
-    n, layout, numel,
-    owners, master, moment, second, average, bucket, squares, w_raw,
-    w_out, master_out, moment_out, second_out, average_out,
-    w_sem,
-):
-    w_copy = pltpu.make_async_copy(w_raw, w_out.at[0], w_sem)
-    w_copy.start()
-    me = lax.axis_index("dp")
-    slot_rows, width = master.shape[2:]
-    cw = width // n
+    loads[3].wait()
     used_rows = jnp.int32(0)
     decay = jnp.float32(0.0)
     for t, (start, count, flag) in enumerate(layout):
@@ -221,20 +209,39 @@
         used_rows = jnp.where(mine, count, used_rows)
         decay = jnp.where(mine, flag, decay)
     used = lax.broadcasted_iota(jnp.int32, (slot_rows, cw), 0) < used_rows
-    factor = clip_factor(squares[...], numel)
     for j in range(n):
-        at = (0, 0, slice(None), slice(j * cw, (j + 1) * cw))
-        grad = unfold(bucket[j].astype(f32))
-        fresh = adam_master(grad, master[at], moment[at], second[at], decay, factor)
-        kept = [
-            jnp.where(used, new, old[at]) for new, old in zip(fresh, (master, moment, second))
-        ]
-        master_out[at] = kept[0]
-        moment_out[at] = kept[1]
-        second_out[at] = kept[2]
-        blended = average_keep * average[at] + (1.0 - average_keep) * kept[0]
-        average_out[at] = jnp.where(used, blended, average[at])
-    w_copy.wait()
+        at = slice(j * cw, (j + 1) * cw)
+        old = [state[k, :, at] for k in range(4)]
+        fresh = adam_master(unfold(bk_recv[j].astype(f32)), old[0], old[1], old[2], decay, factor)
+        blended = average_keep * old[3] + (1.0 - average_keep) * fresh[0]
+        for k, new in enumerate(fresh + (blended,)):
+            state[k, :, at] = jnp.where(used, new, old[k])
+    stores = [
+        pltpu.make_async_copy(state.at[k], ref.at[0, 0], local_sem.at[k])
+        for k, ref in enumerate((master_out, moment_out, second_out, average_out))
+    ]
+    for copy in stores:
+        copy.start()
+
+    for d in range(1, n):
+        there = w_out.at[:, cols(before(d))]
+        pltpu.make_async_copy(there, there, w_sems.at[1, d]).wait()
+    for copy in g_copies + st_copies + q_copies + bk_copies + s_copies + w_copies:
+        copy.wait_send()
+    for copy in stores + [w_own]:
+        copy.wait()
+
+
+def hand_out(*refs):
+    sources, results, sems = refs[:5], refs[5:10], refs[10]
+    copies = [
+        pltpu.make_async_copy(source, result.at[0] if k == 0 else result, sems.at[k])
+        for k, (source, result) in enumerate(zip(sources, results))
+    ]
+    for copy in copies:
+        copy.start()
+    for copy in copies:
+        copy.wait()
 
 
 def local(grads, owners, master, moment, second, average):
@@ -246,50 +253,47 @@
     layout = tensor_layout(rows, slot_rows, owners.shape[1] // 6)
     tensors = len(layout)
     numel = ns * rows * width
-    vmem = pl.BlockSpec(memory_space=pltpu.VMEM)
-    smem = pl.BlockSpec(memory_space=pltpu.SMEM)
-    anywhere = pl.BlockSpec(memory_space=pl.ANY)
+    hbm = pl.BlockSpec(memory_space=pl.ANY)
     packed = (n, 2 * slot_rows, cw // 2)
     sems = lambda count: pltpu.SemaphoreType.DMA((2, count))
-    w_raw, bucket, squares = pl.pallas_call(
+    state = jax.ShapeDtypeStruct(master.shape, f32)
+    results = pl.pallas_call(
         functools.partial(exchange, n, ns, layout, numel),
-        out_shape=(
-            jax.ShapeDtypeStruct((rows, width), bf16),
-            jax.ShapeDtypeStruct(packed, bf16),
-            jax.ShapeDtypeStruct((slot_rows, 128), f32),
-        ),
-        in_specs=[anywhere, smem, anywhere, anywhere, anywhere],
-        out_specs=(vmem, vmem, vmem),
+        out_shape=(jax.ShapeDtypeStruct((rows, width), bf16), state, state, state, state),
+        in_specs=[hbm] * 6,
+        out_specs=(hbm,) * 5,
         scratch_shapes=[
-            pltpu.VMEM((3, slot_rows, width), f32),
+            pltpu.SMEM(owners.shape, jnp.int32),
+            pltpu.VMEM((4, slot_rows, width), f32),
             pltpu.VMEM((n, 6 * slot_rows, cw // 2), bf16),
             pltpu.VMEM((n, 6 * slot_rows, cw // 2), bf16),
             pltpu.VMEM((n, rows, cw), bf16),
             pltpu.VMEM((tensors + 1, slot_rows, cw), f32),
             pltpu.VMEM(packed, bf16),
+            pltpu.VMEM(packed, bf16),
             pltpu.VMEM((rows, cw), f32),
+            pltpu.VMEM((rows, cw), bf16),
             pltpu.VMEM((slot_rows, 128), f32),
             pltpu.VMEM((n, slot_rows, 128), f32),
             pltpu.VMEM((slot_rows, 128), f32),
             pltpu.VMEM((ns, slot_rows, 128), f32),
-            pltpu.SemaphoreType.DMA((4,)),
+            pltpu.SemaphoreType.DMA((7,)),
             sems(n), sems(n), sems(n), sems(n), sems(ns), sems(n),
         ],
         compiler_params=pltpu.CompilerParams(
-            collective_id=0, has_side_effects=True, vmem_limit_bytes=24 * 2**20
+            collective_id=0, has_side_effects=True, vmem_limit_bytes=60 * 2**20
         ),
         name="exchange",
-    )(grads, owners, master, moment, second)
-    state = jax.ShapeDtypeStruct(master.shape, f32)
+    )(grads, owners, master, moment, second, average)
     return pl.pallas_call(
-        functools.partial(update, n, layout, numel),
+        hand_out,
         out_shape=(jax.ShapeDtypeStruct((1, rows, width), bf16), state, state, state, state),
-        in_specs=[smem, vmem, vmem, vmem, vmem, vmem, vmem, anywhere],
-        out_specs=(anywhere, vmem, vmem, vmem, vmem),
-        scratch_shapes=[pltpu.SemaphoreType.DMA],
-        compiler_params=pltpu.CompilerParams(vmem_limit_bytes=24 * 2**20),
-        name="update",
-    )(owners, master, moment, second, average, bucket, squares, w_raw)
+        in_specs=[hbm] * 5,
+        out_specs=(hbm,) * 5,
+        scratch_shapes=[pltpu.SemaphoreType.DMA((5,))],
+        compiler_params=pltpu.CompilerParams(vmem_limit_bytes=60 * 2**20),
+        name="hand_out",
+    )(*results)
 
 
 def solution(mesh):

time: 34.9 us -> 71.1 us (2.04)
  Pallas kernels: 29.4 us -> 70.2 us
  local copies, waits for them, and re-layouts: 4.51 us -> 0 us
    pallas_call x1, Pallas kernels: 2.26 us -> 44.8 us  [local(): pl.pallas_call(hand_out, out_shape=(jax.ShapeDtypeStruct((1, rows, width)...]
    unnamed x18 -> x0, local copies, waits for them, and re-layouts: 4.51 us -> none
    pallas_call x1, Pallas kernels: 27.2 us -> 25.4 us  [local(): pl.pallas_call(functools.partial(exchange, n, ns, layout, numel), out_sha...]
where the time goes in v2:
time: 71.1 us; the launch traced here: 70.8 us
  Pallas kernels  70.2 us (99%)
    pallas_call x1, Pallas kernels, local(): pl.pallas_call(hand_out, out_shape=(jax.ShapeDtypeStruct((1, rows, width)...  44.8 us
    pallas_call x1, Pallas kernels, local(): pl.pallas_call(functools.partial(exchange, n, ns, layout, numel), out_sha...  25.4 us

profile of v2, /device:TPU:0, one launch (start us, length us, event | category | flops | bytes accessed | tf_op | source)
XLA Modules:
  0.0 70.8 jit_solution(17951973702268563137)
XLA Ops:
  0.6 25.4 %exchange.1 = (bf16[20,8192]{1,0:T(8,128)(2,1)}, f32[1,1,8,8192]{3,2,1,0:T(8,128)}, f32[1,1,8,8192]{3,2,1,0:T(8,128)}, f32[1,1,8,8192]{3,2,1,0:T(8,128)}, f32[1,1,8,8192]{3,2,1,0:T(8,128)}) custom-call(bf16[1,1,20,8192]{3,2,1,0:T(8,128)(2,1)} %grads.1, s32[1,6]{1,0:T(1,128)} %owners_hbm.1, f32[1,1,8,8192]{3,2,1,0:T(8,128)} %master.1, ...), custom_call_target="tpu_custom_call" | custom-call | tf_op jit(solution)/shard_map/exchange/pallas_call | solution.py:260
  26.0 44.8 %hand_out.1 = (bf16[1,20,8192]{2,1,0:T(8,128)(2,1)}, f32[1,1,8,8192]{3,2,1,0:T(8,128)}, f32[1,1,8,8192]{3,2,1,0:T(8,128)}, f32[1,1,8,8192]{3,2,1,0:T(8,128)}, f32[1,1,8,8192]{3,2,1,0:T(8,128)}) custom-call(bf16[20,8192]{1,0:T(8,128)(2,1)} %get-tuple-element.10.refs_0_, f32[1,1,8,8192]{3,2,1,0:T(8,128)} %get-tuple-element.11.refs_1_, ...), custom_call_target="tpu_custom_call" | custom-call | tf_op jit(solution)/shard_map/hand_out/pallas_call | solution.py:288

commit v3 on v2

--- a/solution.py
+++ b/solution.py
@@ -42,8 +42,8 @@
     second_new = beta_two * second + (1.0 - beta_two) * clipped * clipped
     direction = (
         moment_new
-        / (1.0 - beta_one**STEP)
-        / (jnp.sqrt(second_new / (1.0 - beta_two**STEP)) + epsilon)
+        * (1.0 / (1.0 - beta_one**STEP))
+        / (jnp.sqrt(second_new * (1.0 / (1.0 - beta_two**STEP))) + epsilon)
     )
     master_new = master - learn_rate * (direction + decay_rate * decay * master)
     return master_new, moment_new, second_new
@@ -68,8 +68,8 @@
     n, ns, layout, numel,
     grads, owners_hbm, master, moment, second, average,
     w_out, master_out, moment_out, second_out, average_out,
-    owners, state, st_send, st_recv, g_recv, tot, bk_send, bk_recv, w_rows, w_send, q_send, q_recv, s_send, s_recv,
-    local_sem, g_sems, st_sems, bk_sems, q_sems, s_sems, w_sems,
+    owners, state, st_send, st_recv, g_mine, g_pair, g_send, g_recv, tot, bk_send, bk_recv, w_rows, w_send, q_send, q_recv, s_send, s_recv,
+    local_sem, load_sem, pair_sems, g_sems, st_sems, st2_sems, bk_sems, q_sems, s_sems, w_sems, fw_sems,
 ):
     me = lax.axis_index("dp")
     sec = lax.axis_index("section")
@@ -77,6 +77,12 @@
     cw = width // n
     slot_rows = state.shape[1]
     tensors = len(layout)
+    chips = n // 2
+    core = lax.rem(me, 2)
+    sibling = me + 1 - 2 * core
+
+    def same_core(index, e):
+        return lax.rem(index + 2 * e, n)
 
     def after(d):
         return lax.rem(me + d, n)
@@ -91,12 +97,15 @@
         pltpu.make_async_copy(ref.at[0, 0], state.at[k], local_sem.at[k])
         for k, ref in enumerate((master, moment, second, average))
     ]
-    own = pltpu.make_async_copy(grads.at[0, 0, :, cols(me)], g_recv.at[0], local_sem.at[4])
-    own_owners = pltpu.make_async_copy(owners_hbm, owners, local_sem.at[5])
-    for copy in loads:
+    own_owners = pltpu.make_async_copy(owners_hbm, owners, local_sem.at[4])
+    own = [
+        pltpu.make_async_copy(
+            grads.at[0, 0, :, cols(same_core(me, e))], g_mine.at[e], load_sem.at[e]
+        )
+        for e in range(chips)
+    ]
+    for copy in loads + own + [own_owners]:
         copy.start()
-    own.start()
-    own_owners.start()
 
     barrier = pltpu.get_barrier_semaphore()
     for d in range(1, n):
@@ -105,6 +114,15 @@
         pl.semaphore_signal(
             barrier, inc=1, device_id={"section": lax.rem(sec + e, ns)}, device_id_type=MESH
         )
+    for copy in loads[:3]:
+        copy.wait()
+    for d in range(n):
+        place = st_recv if d == 0 else st_send
+        for k in range(3):
+            place[d, 2 * slot_rows * k : 2 * slot_rows * (k + 1), :] = fold(state[k, :, cols(after(d))])
+    own_owners.wait()
+    for copy in own:
+        copy.wait()
     pl.semaphore_wait(barrier, n - 1 + ns - 1)
 
     def remote(src, dst, sems, d, target):
@@ -119,24 +137,33 @@
         copy.start()
         return copy
 
-    g_copies = [
-        remote(grads.at[0, 0, :, cols(after(d))], g_recv.at[d], g_sems, d, {"dp": after(d)})
+    pair_copies = [
+        remote(
+            grads.at[0, 0, :, cols(same_core(sibling, e))], g_pair.at[e], pair_sems, e, {"dp": sibling}
+        )
+        for e in [*range(1, chips), 0]
+    ]
+
+    first = pl.ds(0, 2 * slot_rows)
+    others = pl.ds(2 * slot_rows, 4 * slot_rows)
+    st_copies = [
+        remote(st_send.at[d, first], st_recv.at[d, first], st_sems, d, {"dp": after(d)})
         for d in range(1, n)
     ]
 
-    for copy in loads[:3]:
-        copy.wait()
-    for d in range(n):
-        place = st_recv if d == 0 else st_send
-        for k in range(3):
-            place[d, 2 * slot_rows * k : 2 * slot_rows * (k + 1), :] = fold(state[k, :, cols(after(d))])
-    own_owners.wait()
-
-    own.wait()
-    total = g_recv[0].astype(f32)
-    for d, copy in zip(range(1, n), g_copies):
-        copy.wait_recv()
-        total = total + g_recv[d].astype(f32)
+    g_copies = []
+    for e, copy in zip([*range(1, chips), 0], pair_copies):
+        copy.wait_recv()
+        pair = g_mine[e].astype(f32) + g_pair[e].astype(f32)
+        if e:
+            g_send[e] = pair.astype(bf16)
+            g_copies.append(
+                remote(g_send.at[e], g_recv.at[e], g_sems, e, {"dp": same_core(me, e)})
+            )
+    total = pair
+    for e, copy in zip(range(1, chips), g_copies):
+        copy.wait_recv()
+        total = total + g_recv[e].astype(f32)
     mean = total / n
     part = jnp.zeros((slot_rows, 128), f32)
     for t, (start, count, flag) in enumerate(layout):
@@ -153,8 +180,9 @@
         remote(q_send, q_recv.at[d], q_sems, d, {"dp": after(d)}) for d in range(1, n)
     ]
 
-    st_copies = [
-        remote(st_send.at[d], st_recv.at[d], st_sems, d, {"dp": after(d)}) for d in range(1, n)
+    st_copies += [
+        remote(st_send.at[d, others], st_recv.at[d, others], st2_sems, d, {"dp": after(d)})
+        for d in range(1, n)
     ]
 
     bk_copies = []
@@ -194,8 +222,11 @@
         w_rows[start : start + count, :] = fresh[:count]
     w_send[...] = w_rows[...].astype(bf16)
     here = w_out.at[:, cols(me)]
-    w_copies = [remote(w_send, here, w_sems, d, {"dp": after(d)}) for d in range(1, n)]
-    w_own = pltpu.make_async_copy(w_send, here, local_sem.at[6])
+    w_copies = [
+        remote(w_send, here, w_sems, e, {"dp": same_core(me, e)}) for e in range(1, chips)
+    ]
+    w_copies.append(remote(w_send, here, fw_sems, 0, {"dp": sibling}))
+    w_own = pltpu.make_async_copy(w_send, here, local_sem.at[5])
     w_own.start()
 
     for d in range(1, n):
@@ -223,24 +254,33 @@
     for copy in stores:
         copy.start()
 
-    for d in range(1, n):
-        there = w_out.at[:, cols(before(d))]
-        pltpu.make_async_copy(there, there, w_sems.at[1, d]).wait()
-    for copy in g_copies + st_copies + q_copies + bk_copies + s_copies + w_copies:
+    for e in range(1, chips):
+        there = w_out.at[:, cols(same_core(me, chips - e))]
+        pltpu.make_async_copy(there, there, w_sems.at[1, e]).wait()
+        w_copies.append(remote(there, there, fw_sems, e, {"dp": sibling}))
+    for e in range(chips):
+        there = w_out.at[:, cols(same_core(sibling, chips - e))]
+        pltpu.make_async_copy(there, there, fw_sems.at[1, e]).wait()
+    for copy in pair_copies + g_copies + st_copies + q_copies + bk_copies + s_copies + w_copies:
         copy.wait_send()
     for copy in stores + [w_own]:
         copy.wait()
 
 
 def hand_out(*refs):
-    sources, results, sems = refs[:5], refs[5:10], refs[10]
-    copies = [
-        pltpu.make_async_copy(source, result.at[0] if k == 0 else result, sems.at[k])
-        for k, (source, result) in enumerate(zip(sources, results))
-    ]
-    for copy in copies:
+    sources, results, places, sems = refs[:5], refs[5:10], refs[10:15], refs[15]
+    loads = [
+        pltpu.make_async_copy(source, place, sems.at[0, k])
+        for k, (source, place) in enumerate(zip(sources, places))
+    ]
+    for copy in loads:
         copy.start()
-    for copy in copies:
+    stores = []
+    for k, (place, result) in enumerate(zip(places, results)):
+        loads[k].wait()
+        stores.append(pltpu.make_async_copy(place, result.at[0] if k == 0 else result, sems.at[1, k]))
+        stores[-1].start()
+    for copy in stores:
         copy.wait()
 
 
@@ -267,7 +307,7 @@
             pltpu.VMEM((4, slot_rows, width), f32),
             pltpu.VMEM((n, 6 * slot_rows, cw // 2), bf16),
             pltpu.VMEM((n, 6 * slot_rows, cw // 2), bf16),
-            pltpu.VMEM((n, rows, cw), bf16),
+            *[pltpu.VMEM((n // 2, rows, cw), bf16)] * 4,
             pltpu.VMEM((tensors + 1, slot_rows, cw), f32),
             pltpu.VMEM(packed, bf16),
             pltpu.VMEM(packed, bf16),
@@ -277,8 +317,10 @@
             pltpu.VMEM((n, slot_rows, 128), f32),
             pltpu.VMEM((slot_rows, 128), f32),
             pltpu.VMEM((ns, slot_rows, 128), f32),
-            pltpu.SemaphoreType.DMA((7,)),
-            sems(n), sems(n), sems(n), sems(n), sems(ns), sems(n),
+            pltpu.SemaphoreType.DMA((6,)),
+            pltpu.SemaphoreType.DMA((n // 2,)),
+            sems(n // 2), sems(n // 2), sems(n), sems(n), sems(n), sems(n), sems(ns),
+            sems(n // 2), sems(n // 2),
         ],
         compiler_params=pltpu.CompilerParams(
             collective_id=0, has_side_effects=True, vmem_limit_bytes=60 * 2**20
@@ -290,7 +332,11 @@
         out_shape=(jax.ShapeDtypeStruct((1, rows, width), bf16), state, state, state, state),
         in_specs=[hbm] * 5,
         out_specs=(hbm,) * 5,
-        scratch_shapes=[pltpu.SemaphoreType.DMA((5,))],
+        scratch_shapes=[
+            pltpu.VMEM((rows, width), bf16),
+            *[pltpu.VMEM(master.shape, f32)] * 4,
+            pltpu.SemaphoreType.DMA((2, 5)),
+        ],
         compiler_params=pltpu.CompilerParams(vmem_limit_bytes=60 * 2**20),
         name="hand_out",
     )(*results)

time: 71.1 us -> 27.3 us (0.38)
  Pallas kernels: 70.2 us -> 26.5 us
    pallas_call x1, Pallas kernels: 44.8 us -> 2.17 us  [local(): pl.pallas_call(hand_out, out_shape=(jax.ShapeDtypeStruct((1, rows, width)...]
    pallas_call x1, Pallas kernels: 25.4 us -> 24.3 us  [local(): pl.pallas_call(functools.partial(exchange, n, ns, layout, numel), out_sha...]
where the time goes in v3:
time: 27.3 us; the launch traced here: 27.1 us
  Pallas kernels  26.5 us (97%)
  between operations  0.64 us (2%)
    pallas_call x1, Pallas kernels, local(): pl.pallas_call(functools.partial(exchange, n, ns, layout, numel), out_sha...  24.3 us
    pallas_call x1, Pallas kernels, local(): pl.pallas_call(hand_out, out_shape=(jax.ShapeDtypeStruct((1, rows, width)...  2.17 us

profile of v3, /device:TPU:0, one launch (start us, length us, event | category | flops | bytes accessed | tf_op | source)
XLA Modules:
  0.0 27.1 jit_solution(7525538457667196365)
XLA Ops:
  0.6 24.3 %exchange.1 = (bf16[20,8192]{1,0:T(8,128)(2,1)}, f32[1,1,8,8192]{3,2,1,0:T(8,128)}, f32[1,1,8,8192]{3,2,1,0:T(8,128)}, f32[1,1,8,8192]{3,2,1,0:T(8,128)}, f32[1,1,8,8192]{3,2,1,0:T(8,128)}) custom-call(bf16[1,1,20,8192]{3,2,1,0:T(8,128)(2,1)} %grads.1, s32[1,6]{1,0:T(1,128)} %owners_hbm.1, f32[1,1,8,8192]{3,2,1,0:T(8,128)} %master.1, ...), custom_call_target="tpu_custom_call" | custom-call | tf_op jit(solution)/shard_map/exchange/pallas_call | solution.py:300
  25.0 2.2 %hand_out.1 = (bf16[1,20,8192]{2,1,0:T(8,128)(2,1)}, f32[1,1,8,8192]{3,2,1,0:T(8,128)}, f32[1,1,8,8192]{3,2,1,0:T(8,128)}, f32[1,1,8,8192]{3,2,1,0:T(8,128)}, f32[1,1,8,8192]{3,2,1,0:T(8,128)}) custom-call(bf16[20,8192]{1,0:T(8,128)(2,1)} %get-tuple-element.10.refs_0_, f32[1,1,8,8192]{3,2,1,0:T(8,128)} %get-tuple-element.11.refs_1_, ...), custom_call_target="tpu_custom_call" | custom-call | tf_op jit(solution)/shard_map/hand_out/pallas_call | solution.py:330

commit v4 on v3

--- a/solution.py
+++ b/solution.py
@@ -68,7 +68,7 @@
     n, ns, layout, numel,
     grads, owners_hbm, master, moment, second, average,
     w_out, master_out, moment_out, second_out, average_out,
-    owners, state, st_send, st_recv, g_mine, g_pair, g_send, g_recv, tot, bk_send, bk_recv, w_rows, w_send, q_send, q_recv, s_send, s_recv,
+    owners, state, st_send, st_recv, g_mine, g_pair, g_send, g_recv, tot, bk_send, bk_recv, mean_rows, old_rows, w_send, q_send, q_recv, s_send, s_recv,
     local_sem, load_sem, pair_sems, g_sems, st_sems, st2_sems, bk_sems, q_sems, s_sems, w_sems, fw_sems,
 ):
     me = lax.axis_index("dp")
@@ -114,15 +114,6 @@
         pl.semaphore_signal(
             barrier, inc=1, device_id={"section": lax.rem(sec + e, ns)}, device_id_type=MESH
         )
-    for copy in loads[:3]:
-        copy.wait()
-    for d in range(n):
-        place = st_recv if d == 0 else st_send
-        for k in range(3):
-            place[d, 2 * slot_rows * k : 2 * slot_rows * (k + 1), :] = fold(state[k, :, cols(after(d))])
-    own_owners.wait()
-    for copy in own:
-        copy.wait()
     pl.semaphore_wait(barrier, n - 1 + ns - 1)
 
     def remote(src, dst, sems, d, target):
@@ -146,11 +137,20 @@
 
     first = pl.ds(0, 2 * slot_rows)
     others = pl.ds(2 * slot_rows, 4 * slot_rows)
+    def pack(k):
+        loads[k].wait()
+        for d in range(n):
+            place = st_recv if d == 0 else st_send
+            place[d, 2 * slot_rows * k : 2 * slot_rows * (k + 1), :] = fold(state[k, :, cols(after(d))])
+
+    pack(0)
     st_copies = [
         remote(st_send.at[d, first], st_recv.at[d, first], st_sems, d, {"dp": after(d)})
         for d in range(1, n)
     ]
 
+    for copy in own:
+        copy.wait()
     g_copies = []
     for e, copy in zip([*range(1, chips), 0], pair_copies):
         copy.wait_recv()
@@ -160,29 +160,49 @@
             g_copies.append(
                 remote(g_send.at[e], g_recv.at[e], g_sems, e, {"dp": same_core(me, e)})
             )
+    pack(1)
+    pack(2)
+    own_owners.wait()
     total = pair
     for e, copy in zip(range(1, chips), g_copies):
         copy.wait_recv()
         total = total + g_recv[e].astype(f32)
     mean = total / n
+    mean_rows[...] = mean
     part = jnp.zeros((slot_rows, 128), f32)
+    for r in range(0, rows, slot_rows):
+        piece = mean[r : r + slot_rows]
+        for c in range(0, cw, 128):
+            square = piece[:, c : c + 128] * piece[:, c : c + 128]
+            if len(square) < slot_rows:
+                lacking = jnp.zeros((slot_rows - len(square), 128), f32)
+                square = jnp.concatenate([square, lacking], axis=0)
+            part = part + square
+
+    q_send[...] = part
+    q_copies = [
+        remote(q_send, q_recv.at[d], q_sems, d, {"dp": after(d)}) for d in range(1, n)
+    ]
+
+    st_copies += [
+        remote(st_send.at[d, others], st_recv.at[d, others], st2_sems, d, {"dp": after(d)})
+        for d in range(1, n)
+    ]
+
     for t, (start, count, flag) in enumerate(layout):
-        piece = mean[start : start + count]
+        piece = mean_rows[start : start + count, :]
         if count < slot_rows:
             piece = jnp.concatenate([piece, jnp.zeros((slot_rows - count, cw), f32)], axis=0)
         tot[t] = piece
-        for c in range(0, cw, 128):
-            part = part + piece[:, c : c + 128] * piece[:, c : c + 128]
     tot[tensors] = jnp.zeros((slot_rows, cw), f32)
 
-    q_send[...] = part
-    q_copies = [
-        remote(q_send, q_recv.at[d], q_sems, d, {"dp": after(d)}) for d in range(1, n)
-    ]
-
-    st_copies += [
-        remote(st_send.at[d, others], st_recv.at[d, others], st2_sems, d, {"dp": after(d)})
-        for d in range(1, n)
+    for d, copy in zip(range(1, n), q_copies):
+        copy.wait_recv()
+        part = part + q_recv[d]
+    s_send[...] = part
+    s_copies = [
+        remote(s_send, s_recv.at[e], s_sems, e, {"section": lax.rem(sec + e, ns)})
+        for e in range(1, ns)
     ]
 
     bk_copies = []
@@ -200,27 +220,24 @@
                 remote(bk_send.at[d], bk_recv.at[me], bk_sems, d, {"dp": target})
             )
 
-    for d, copy in zip(range(1, n), q_copies):
-        copy.wait_recv()
-        part = part + q_recv[d]
-    s_send[...] = part
-    s_copies = [
-        remote(s_send, s_recv.at[e], s_sems, e, {"section": lax.rem(sec + e, ns)})
-        for e in range(1, ns)
-    ]
+    for copy in st_copies:
+        copy.wait_recv()
+    row = lax.broadcasted_iota(jnp.int32, (rows, cw), 0)
+    decays = jnp.zeros((rows, cw), f32)
+    for t, (start, count, flag) in enumerate(layout):
+        olds = st_recv[lax.rem(me - owners[0, t] + n, n)].astype(f32)
+        for k in range(3):
+            old = unfold(olds[2 * slot_rows * k : 2 * slot_rows * (k + 1)])
+            old_rows[k, start : start + count, :] = old[:count]
+        if flag:
+            decays = jnp.where(jnp.logical_and(row >= start, row < start + count), flag, decays)
+
     for e, copy in zip(range(1, ns), s_copies):
         copy.wait_recv()
         part = part + s_recv[e]
     factor = clip_factor(part, numel)
-
-    for copy in st_copies:
-        copy.wait_recv()
-    for t, (start, count, flag) in enumerate(layout):
-        olds = st_recv[lax.rem(me - owners[0, t] + n, n)].astype(f32)
-        old = [unfold(olds[2 * slot_rows * k : 2 * slot_rows * (k + 1)]) for k in range(3)]
-        fresh, _, _ = adam_master(tot[t], old[0], old[1], old[2], flag, factor)
-        w_rows[start : start + count, :] = fresh[:count]
-    w_send[...] = w_rows[...].astype(bf16)
+    fresh, _, _ = adam_master(mean_rows[...], old_rows[0], old_rows[1], old_rows[2], decays, factor)
+    w_send[...] = fresh.astype(bf16)
     here = w_out.at[:, cols(me)]
     w_copies = [
         remote(w_send, here, w_sems, e, {"dp": same_core(me, e)}) for e in range(1, chips)
@@ -254,6 +271,9 @@
     for copy in stores:
         copy.start()
 
+    for copy in pair_copies + g_copies + st_copies + q_copies + s_copies + bk_copies:
+        copy.wait_send()
+
     for e in range(1, chips):
         there = w_out.at[:, cols(same_core(me, chips - e))]
         pltpu.make_async_copy(there, there, w_sems.at[1, e]).wait()
@@ -261,7 +281,7 @@
     for e in range(chips):
         there = w_out.at[:, cols(same_core(sibling, chips - e))]
         pltpu.make_async_copy(there, there, fw_sems.at[1, e]).wait()
-    for copy in pair_copies + g_copies + st_copies + q_copies + bk_copies + s_copies + w_copies:
+    for copy in w_copies:
         copy.wait_send()
     for copy in stores + [w_own]:
         copy.wait()
@@ -312,6 +332,7 @@
             pltpu.VMEM(packed, bf16),
             pltpu.VMEM(packed, bf16),
             pltpu.VMEM((rows, cw), f32),
+            pltpu.VMEM((3, rows, cw), f32),
             pltpu.VMEM((rows, cw), bf16),
             pltpu.VMEM((slot_rows, 128), f32),
             pltpu.VMEM((n, slot_rows, 128), f32),

time: 27.3 us -> 27.1 us (level)
  no operation moved by 1% of the time
where the time goes in v4:
time: 27.1 us; the launch traced here: 27 us
  Pallas kernels  26.3 us (97%)
  between operations  0.64 us (2%)
    pallas_call x1, Pallas kernels, local(): pl.pallas_call(functools.partial(exchange, n, ns, layout, numel), out_sha...  24.2 us
    pallas_call x1, Pallas kernels, local(): pl.pallas_call(hand_out, out_shape=(jax.ShapeDtypeStruct((1, rows, width)...  2.17 us

profile of v4, /device:TPU:0, one launch (start us, length us, event | category | flops | bytes accessed | tf_op | source)
XLA Modules:
  0.0 27.0 jit_solution(8068235506979678565)
XLA Ops:
  0.6 24.2 %exchange.1 = (bf16[20,8192]{1,0:T(8,128)(2,1)}, f32[1,1,8,8192]{3,2,1,0:T(8,128)}, f32[1,1,8,8192]{3,2,1,0:T(8,128)}, f32[1,1,8,8192]{3,2,1,0:T(8,128)}, f32[1,1,8,8192]{3,2,1,0:T(8,128)}) custom-call(bf16[1,1,20,8192]{3,2,1,0:T(8,128)(2,1)} %grads.1, s32[1,6]{1,0:T(1,128)} %owners_hbm.1, f32[1,1,8,8192]{3,2,1,0:T(8,128)} %master.1, ...), custom_call_target="tpu_custom_call" | custom-call | tf_op jit(solution)/shard_map/exchange/pallas_call | solution.py:320
  24.8 2.2 %hand_out.1 = (bf16[1,20,8192]{2,1,0:T(8,128)(2,1)}, f32[1,1,8,8192]{3,2,1,0:T(8,128)}, f32[1,1,8,8192]{3,2,1,0:T(8,128)}, f32[1,1,8,8192]{3,2,1,0:T(8,128)}, f32[1,1,8,8192]{3,2,1,0:T(8,128)}) custom-call(bf16[20,8192]{1,0:T(8,128)(2,1)} %get-tuple-element.10.refs_0_, f32[1,1,8,8192]{3,2,1,0:T(8,128)} %get-tuple-element.11.refs_1_, ...), custom_call_target="tpu_custom_call" | custom-call | tf_op jit(solution)/shard_map/hand_out/pallas_call | solution.py:351

commit v5 on v4

--- a/solution.py
+++ b/solution.py
@@ -68,7 +68,7 @@
     n, ns, layout, numel,
     grads, owners_hbm, master, moment, second, average,
     w_out, master_out, moment_out, second_out, average_out,
-    owners, state, st_send, st_recv, g_mine, g_pair, g_send, g_recv, tot, bk_send, bk_recv, mean_rows, old_rows, w_send, q_send, q_recv, s_send, s_recv,
+    owners, state, st_send, st_recv, g_mine, g_pair, g_send, g_recv, tot, bk_send, bk_recv, mean_rows, old_rows, w_send, w_recv, q_send, q_recv, s_send, s_recv,
     local_sem, load_sem, pair_sems, g_sems, st_sems, st2_sems, bk_sems, q_sems, s_sems, w_sems, fw_sems,
 ):
     me = lax.axis_index("dp")
@@ -240,11 +240,11 @@
     w_send[...] = fresh.astype(bf16)
     here = w_out.at[:, cols(me)]
     w_copies = [
-        remote(w_send, here, w_sems, e, {"dp": same_core(me, e)}) for e in range(1, chips)
+        remote(w_send, w_recv.at[e], w_sems, e, {"dp": same_core(me, e)}) for e in range(1, chips)
     ]
     w_copies.append(remote(w_send, here, fw_sems, 0, {"dp": sibling}))
-    w_own = pltpu.make_async_copy(w_send, here, local_sem.at[5])
-    w_own.start()
+    w_stores = [pltpu.make_async_copy(w_send, here, load_sem.at[0])]
+    w_stores[0].start()
 
     for d in range(1, n):
         place = bk_recv.at[before(d)]
@@ -276,14 +276,16 @@
 
     for e in range(1, chips):
         there = w_out.at[:, cols(same_core(me, chips - e))]
-        pltpu.make_async_copy(there, there, w_sems.at[1, e]).wait()
-        w_copies.append(remote(there, there, fw_sems, e, {"dp": sibling}))
+        w_copies[e - 1].wait_recv()
+        w_copies.append(remote(w_recv.at[e], there, fw_sems, e, {"dp": sibling}))
+        w_stores.append(pltpu.make_async_copy(w_recv.at[e], there, load_sem.at[e]))
+        w_stores[-1].start()
     for e in range(chips):
         there = w_out.at[:, cols(same_core(sibling, chips - e))]
         pltpu.make_async_copy(there, there, fw_sems.at[1, e]).wait()
     for copy in w_copies:
         copy.wait_send()
-    for copy in stores + [w_own]:
+    for copy in stores + w_stores:
         copy.wait()
 
 
@@ -334,11 +336,12 @@
             pltpu.VMEM((rows, cw), f32),
             pltpu.VMEM((3, rows, cw), f32),
             pltpu.VMEM((rows, cw), bf16),
+            pltpu.VMEM((n // 2, rows, cw), bf16),
             pltpu.VMEM((slot_rows, 128), f32),
             pltpu.VMEM((n, slot_rows, 128), f32),
             pltpu.VMEM((slot_rows, 128), f32),
             pltpu.VMEM((ns, slot_rows, 128), f32),
-            pltpu.SemaphoreType.DMA((6,)),
+            pltpu.SemaphoreType.DMA((5,)),
             pltpu.SemaphoreType.DMA((n // 2,)),
             sems(n // 2), sems(n // 2), sems(n), sems(n), sems(n), sems(n), sems(ns),
             sems(n // 2), sems(n // 2),

time: 27.1 us -> 26.8 us (0.989)
  Pallas kernels: 26.3 us -> 26 us
    pallas_call x1, Pallas kernels: 24.2 us -> 23.9 us  [local(): pl.pallas_call(functools.partial(exchange, n, ns, layout, numel), out_sha...]
where the time goes in v5:
time: 26.8 us; the launch traced here: 26.7 us
  Pallas kernels  26 us (97%)
  between operations  0.64 us (2%)
    pallas_call x1, Pallas kernels, local(): pl.pallas_call(functools.partial(exchange, n, ns, layout, numel), out_sha...  23.9 us
    pallas_call x1, Pallas kernels, local(): pl.pallas_call(hand_out, out_shape=(jax.ShapeDtypeStruct((1, rows, width)...  2.17 us

profile of v5, /device:TPU:0, one launch (start us, length us, event | category | flops | bytes accessed | tf_op | source)
XLA Modules:
  0.0 26.7 jit_solution(5879751978500869774)
XLA Ops:
  0.6 23.9 %exchange.1 = (bf16[20,8192]{1,0:T(8,128)(2,1)}, f32[1,1,8,8192]{3,2,1,0:T(8,128)}, f32[1,1,8,8192]{3,2,1,0:T(8,128)}, f32[1,1,8,8192]{3,2,1,0:T(8,128)}, f32[1,1,8,8192]{3,2,1,0:T(8,128)}) custom-call(bf16[1,1,20,8192]{3,2,1,0:T(8,128)(2,1)} %grads.1, s32[1,6]{1,0:T(1,128)} %owners_hbm.1, f32[1,1,8,8192]{3,2,1,0:T(8,128)} %master.1, ...), custom_call_target="tpu_custom_call" | custom-call | tf_op jit(solution)/shard_map/exchange/pallas_call | solution.py:322
  24.5 2.2 %hand_out.1 = (bf16[1,20,8192]{2,1,0:T(8,128)(2,1)}, f32[1,1,8,8192]{3,2,1,0:T(8,128)}, f32[1,1,8,8192]{3,2,1,0:T(8,128)}, f32[1,1,8,8192]{3,2,1,0:T(8,128)}, f32[1,1,8,8192]{3,2,1,0:T(8,128)}) custom-call(bf16[20,8192]{1,0:T(8,128)(2,1)} %get-tuple-element.10.refs_0_, f32[1,1,8,8192]{3,2,1,0:T(8,128)} %get-tuple-element.11.refs_1_, ...), custom_call_target="tpu_custom_call" | custom-call | tf_op jit(solution)/shard_map/hand_out/pallas_call | solution.py:354

commit v6 on v4

--- a/solution.py
+++ b/solution.py
@@ -68,8 +68,8 @@
     n, ns, layout, numel,
     grads, owners_hbm, master, moment, second, average,
     w_out, master_out, moment_out, second_out, average_out,
-    owners, state, st_send, st_recv, g_mine, g_pair, g_send, g_recv, tot, bk_send, bk_recv, mean_rows, old_rows, w_send, q_send, q_recv, s_send, s_recv,
-    local_sem, load_sem, pair_sems, g_sems, st_sems, st2_sems, bk_sems, q_sems, s_sems, w_sems, fw_sems,
+    owners, state, st_send, st_recv, g_mine, g_pair, g_send, g_recv, tot, bk_send, bk_recv, mean_rows, w_rows, w_send, w_recv, q_send, q_recv, s_send, s_recv,
+    local_sem, load_sem, pair_sems, g_sems, st_sems, bk_sems, q_sems, s_sems, w_sems, fw_sems,
 ):
     me = lax.axis_index("dp")
     sec = lax.axis_index("section")
@@ -135,20 +135,6 @@
         for e in [*range(1, chips), 0]
     ]
 
-    first = pl.ds(0, 2 * slot_rows)
-    others = pl.ds(2 * slot_rows, 4 * slot_rows)
-    def pack(k):
-        loads[k].wait()
-        for d in range(n):
-            place = st_recv if d == 0 else st_send
-            place[d, 2 * slot_rows * k : 2 * slot_rows * (k + 1), :] = fold(state[k, :, cols(after(d))])
-
-    pack(0)
-    st_copies = [
-        remote(st_send.at[d, first], st_recv.at[d, first], st_sems, d, {"dp": after(d)})
-        for d in range(1, n)
-    ]
-
     for copy in own:
         copy.wait()
     g_copies = []
@@ -160,8 +146,6 @@
             g_copies.append(
                 remote(g_send.at[e], g_recv.at[e], g_sems, e, {"dp": same_core(me, e)})
             )
-    pack(1)
-    pack(2)
     own_owners.wait()
     total = pair
     for e, copy in zip(range(1, chips), g_copies):
@@ -184,26 +168,12 @@
         remote(q_send, q_recv.at[d], q_sems, d, {"dp": after(d)}) for d in range(1, n)
     ]
 
-    st_copies += [
-        remote(st_send.at[d, others], st_recv.at[d, others], st2_sems, d, {"dp": after(d)})
-        for d in range(1, n)
-    ]
-
     for t, (start, count, flag) in enumerate(layout):
         piece = mean_rows[start : start + count, :]
         if count < slot_rows:
             piece = jnp.concatenate([piece, jnp.zeros((slot_rows - count, cw), f32)], axis=0)
         tot[t] = piece
     tot[tensors] = jnp.zeros((slot_rows, cw), f32)
-
-    for d, copy in zip(range(1, n), q_copies):
-        copy.wait_recv()
-        part = part + q_recv[d]
-    s_send[...] = part
-    s_copies = [
-        remote(s_send, s_recv.at[e], s_sems, e, {"section": lax.rem(sec + e, ns)})
-        for e in range(1, ns)
-    ]
 
     bk_copies = []
     for d in range(n):
@@ -220,36 +190,20 @@
                 remote(bk_send.at[d], bk_recv.at[me], bk_sems, d, {"dp": target})
             )
 
-    for copy in st_copies:
-        copy.wait_recv()
-    row = lax.broadcasted_iota(jnp.int32, (rows, cw), 0)
-    decays = jnp.zeros((rows, cw), f32)
-    for t, (start, count, flag) in enumerate(layout):
-        olds = st_recv[lax.rem(me - owners[0, t] + n, n)].astype(f32)
-        for k in range(3):
-            old = unfold(olds[2 * slot_rows * k : 2 * slot_rows * (k + 1)])
-            old_rows[k, start : start + count, :] = old[:count]
-        if flag:
-            decays = jnp.where(jnp.logical_and(row >= start, row < start + count), flag, decays)
-
-    for e, copy in zip(range(1, ns), s_copies):
-        copy.wait_recv()
-        part = part + s_recv[e]
-    factor = clip_factor(part, numel)
-    fresh, _, _ = adam_master(mean_rows[...], old_rows[0], old_rows[1], old_rows[2], decays, factor)
-    w_send[...] = fresh.astype(bf16)
-    here = w_out.at[:, cols(me)]
-    w_copies = [
-        remote(w_send, here, w_sems, e, {"dp": same_core(me, e)}) for e in range(1, chips)
-    ]
-    w_copies.append(remote(w_send, here, fw_sems, 0, {"dp": sibling}))
-    w_own = pltpu.make_async_copy(w_send, here, local_sem.at[5])
-    w_own.start()
-
+    for d, copy in zip(range(1, n), q_copies):
+        copy.wait_recv()
+        part = part + q_recv[d]
+    s_send[...] = part
+    s_copies = [
+        remote(s_send, s_recv.at[e], s_sems, e, {"section": lax.rem(sec + e, ns)})
+        for e in range(1, ns)
+    ]
+
+    for copy in loads:
+        copy.wait()
     for d in range(1, n):
         place = bk_recv.at[before(d)]
         pltpu.make_async_copy(place, place, bk_sems.at[1, d]).wait()
-    loads[3].wait()
     used_rows = jnp.int32(0)
     decay = jnp.float32(0.0)
     for t, (start, count, flag) in enumerate(layout):
@@ -257,33 +211,62 @@
         used_rows = jnp.where(mine, count, used_rows)
         decay = jnp.where(mine, flag, decay)
     used = lax.broadcasted_iota(jnp.int32, (slot_rows, cw), 0) < used_rows
-    for j in range(n):
-        at = slice(j * cw, (j + 1) * cw)
+
+    for e, copy in zip(range(1, ns), s_copies):
+        copy.wait_recv()
+        part = part + s_recv[e]
+    factor = clip_factor(part, numel)
+
+    st_copies = []
+    for d in [*range(1, n), 0]:
+        at = cols(after(d))
         old = [state[k, :, at] for k in range(4)]
-        fresh = adam_master(unfold(bk_recv[j].astype(f32)), old[0], old[1], old[2], decay, factor)
+        grad = unfold(bk_recv[after(d)].astype(f32))
+        fresh = adam_master(grad, old[0], old[1], old[2], decay, factor)
         blended = average_keep * old[3] + (1.0 - average_keep) * fresh[0]
-        for k, new in enumerate(fresh + (blended,)):
-            state[k, :, at] = jnp.where(used, new, old[k])
+        kept = [jnp.where(used, new, o) for new, o in zip(fresh + (blended,), old)]
+        if d:
+            st_send[d] = fold(kept[0])
+            st_copies.append(remote(st_send.at[d], st_recv.at[d], st_sems, d, {"dp": after(d)}))
+        else:
+            st_recv[0] = fold(kept[0])
+        for k in range(4):
+            state[k, :, at] = kept[k]
     stores = [
         pltpu.make_async_copy(state.at[k], ref.at[0, 0], local_sem.at[k])
         for k, ref in enumerate((master_out, moment_out, second_out, average_out))
     ]
     for copy in stores:
         copy.start()
+    for copy in st_copies:
+        copy.wait_recv()
+    for t, (start, count, flag) in enumerate(layout):
+        block = unfold(st_recv[lax.rem(me - owners[0, t] + n, n)].astype(f32))
+        w_rows[start : start + count, :] = block[:count]
+    w_send[...] = w_rows[...].astype(bf16)
+    here = w_out.at[:, cols(me)]
+    w_copies = [
+        remote(w_send, w_recv.at[e], w_sems, e, {"dp": same_core(me, e)}) for e in range(1, chips)
+    ]
+    w_copies.append(remote(w_send, here, fw_sems, 0, {"dp": sibling}))
+    w_stores = [pltpu.make_async_copy(w_send, here, load_sem.at[0])]
+    w_stores[0].start()
 
     for copy in pair_copies + g_copies + st_copies + q_copies + s_copies + bk_copies:
         copy.wait_send()
 
     for e in range(1, chips):
         there = w_out.at[:, cols(same_core(me, chips - e))]
-        pltpu.make_async_copy(there, there, w_sems.at[1, e]).wait()
-        w_copies.append(remote(there, there, fw_sems, e, {"dp": sibling}))
+        w_copies[e - 1].wait_recv()
+        w_copies.append(remote(w_recv.at[e], there, fw_sems, e, {"dp": sibling}))
+        w_stores.append(pltpu.make_async_copy(w_recv.at[e], there, load_sem.at[e]))
+        w_stores[-1].start()
     for e in range(chips):
         there = w_out.at[:, cols(same_core(sibling, chips - e))]
         pltpu.make_async_copy(there, there, fw_sems.at[1, e]).wait()
     for copy in w_copies:
         copy.wait_send()
-    for copy in stores + [w_own]:
+    for copy in stores + w_stores:
         copy.wait()
 
 
@@ -325,22 +308,23 @@
         scratch_shapes=[
             pltpu.SMEM(owners.shape, jnp.int32),
             pltpu.VMEM((4, slot_rows, width), f32),
-            pltpu.VMEM((n, 6 * slot_rows, cw // 2), bf16),
-            pltpu.VMEM((n, 6 * slot_rows, cw // 2), bf16),
+            pltpu.VMEM(packed, bf16),
+            pltpu.VMEM(packed, bf16),
             *[pltpu.VMEM((n // 2, rows, cw), bf16)] * 4,
             pltpu.VMEM((tensors + 1, slot_rows, cw), f32),
             pltpu.VMEM(packed, bf16),
             pltpu.VMEM(packed, bf16),
             pltpu.VMEM((rows, cw), f32),
-            pltpu.VMEM((3, rows, cw), f32),
+            pltpu.VMEM((rows, cw), f32),
             pltpu.VMEM((rows, cw), bf16),
+            pltpu.VMEM((n // 2, rows, cw), bf16),
             pltpu.VMEM((slot_rows, 128), f32),
             pltpu.VMEM((n, slot_rows, 128), f32),
             pltpu.VMEM((slot_rows, 128), f32),
             pltpu.VMEM((ns, slot_rows, 128), f32),
-            pltpu.SemaphoreType.DMA((6,)),
+            pltpu.SemaphoreType.DMA((5,)),
             pltpu.SemaphoreType.DMA((n // 2,)),
-            sems(n // 2), sems(n // 2), sems(n), sems(n), sems(n), sems(n), sems(ns),
+            sems(n // 2), sems(n // 2), sems(n), sems(n), sems(n), sems(ns),
             sems(n // 2), sems(n // 2),
         ],
         compiler_params=pltpu.CompilerParams(

time: 27.1 us -> 30.8 us (1.14)
  Pallas kernels: 26.3 us -> 30 us
    pallas_call x1, Pallas kernels: 24.2 us -> 27.9 us  [local(): pl.pallas_call(functools.partial(exchange, n, ns, layout, numel), out_sha...]
where the time goes in v6:
time: 30.8 us; the launch traced here: 30.7 us
  Pallas kernels  30 us (97%)
  between operations  0.64 us (2%)
    pallas_call x1, Pallas kernels, local(): pl.pallas_call(functools.partial(exchange, n, ns, layout, numel), out_sha...  27.9 us
    pallas_call x1, Pallas kernels, local(): pl.pallas_call(hand_out, out_shape=(jax.ShapeDtypeStruct((1, rows, width)...  2.17 us

profile of v6, /device:TPU:0, one launch (start us, length us, event | category | flops | bytes accessed | tf_op | source)
XLA Modules:
  0.0 30.7 jit_solution(8781156463481218705)
XLA Ops:
  0.6 27.9 %exchange.1 = (bf16[20,8192]{1,0:T(8,128)(2,1)}, f32[1,1,8,8192]{3,2,1,0:T(8,128)}, f32[1,1,8,8192]{3,2,1,0:T(8,128)}, f32[1,1,8,8192]{3,2,1,0:T(8,128)}, f32[1,1,8,8192]{3,2,1,0:T(8,128)}) custom-call(bf16[1,1,20,8192]{3,2,1,0:T(8,128)(2,1)} %grads.1, s32[1,6]{1,0:T(1,128)} %owners_hbm.1, f32[1,1,8,8192]{3,2,1,0:T(8,128)} %master.1, ...), custom_call_target="tpu_custom_call" | custom-call | tf_op jit(solution)/shard_map/exchange/pallas_call | solution.py:303
  28.5 2.2 %hand_out.1 = (bf16[1,20,8192]{2,1,0:T(8,128)(2,1)}, f32[1,1,8,8192]{3,2,1,0:T(8,128)}, f32[1,1,8,8192]{3,2,1,0:T(8,128)}, f32[1,1,8,8192]{3,2,1,0:T(8,128)}, f32[1,1,8,8192]{3,2,1,0:T(8,128)}) custom-call(bf16[20,8192]{1,0:T(8,128)(2,1)} %get-tuple-element.10.refs_0_, f32[1,1,8,8192]{3,2,1,0:T(8,128)} %get-tuple-element.11.refs_1_, ...), custom_call_target="tpu_custom_call" | custom-call | tf_op jit(solution)/shard_map/hand_out/pallas_call | solution.py:335

commit v7 on v5

--- a/solution.py
+++ b/solution.py
@@ -68,8 +68,8 @@
     n, ns, layout, numel,
     grads, owners_hbm, master, moment, second, average,
     w_out, master_out, moment_out, second_out, average_out,
-    owners, state, st_send, st_recv, g_mine, g_pair, g_send, g_recv, tot, bk_send, bk_recv, mean_rows, old_rows, w_send, w_recv, q_send, q_recv, s_send, s_recv,
-    local_sem, load_sem, pair_sems, g_sems, st_sems, st2_sems, bk_sems, q_sems, s_sems, w_sems, fw_sems,
+    owners, state, st_send, st_recv, g_mine, g_pair, g_send, g_recv, tot, bk_send, bk_recv, mean_rows, old_rows, w_send, w_recv, q_send, q_recv,
+    local_sem, load_sem, pair_sems, g_sems, st_sems, st2_sems, bk_sems, q_sems, w_sems, fw_sems,
 ):
     me = lax.axis_index("dp")
     sec = lax.axis_index("section")
@@ -108,13 +108,14 @@
         copy.start()
 
     barrier = pltpu.get_barrier_semaphore()
-    for d in range(1, n):
-        pl.semaphore_signal(barrier, inc=1, device_id={"dp": after(d)}, device_id_type=MESH)
-    for e in range(1, ns):
-        pl.semaphore_signal(
-            barrier, inc=1, device_id={"section": lax.rem(sec + e, ns)}, device_id_type=MESH
-        )
-    pl.semaphore_wait(barrier, n - 1 + ns - 1)
+    def other(i):
+        return {"section": lax.rem(sec + i // n, ns), "dp": lax.rem(me + i % n, n)}
+
+    @pl.loop(1, n * ns)
+    def _(i):
+        pl.semaphore_signal(barrier, inc=1, device_id=other(i), device_id_type=MESH)
+
+    pl.semaphore_wait(barrier, n * ns - 1)
 
     def remote(src, dst, sems, d, target):
         copy = pltpu.make_async_remote_copy(
@@ -180,9 +181,20 @@
             part = part + square
 
     q_send[...] = part
-    q_copies = [
-        remote(q_send, q_recv.at[d], q_sems, d, {"dp": after(d)}) for d in range(1, n)
-    ]
+
+    def square_copy(i):
+        return pltpu.make_async_remote_copy(
+            src_ref=q_send,
+            dst_ref=q_recv.at[i],
+            send_sem=q_sems.at[0],
+            recv_sem=q_sems.at[1],
+            device_id=other(i),
+            device_id_type=MESH,
+        )
+
+    @pl.loop(1, n * ns)
+    def _(i):
+        square_copy(i).start()
 
     st_copies += [
         remote(st_send.at[d, others], st_recv.at[d, others], st2_sems, d, {"dp": after(d)})
@@ -195,15 +207,6 @@
             piece = jnp.concatenate([piece, jnp.zeros((slot_rows - count, cw), f32)], axis=0)
         tot[t] = piece
     tot[tensors] = jnp.zeros((slot_rows, cw), f32)
-
-    for d, copy in zip(range(1, n), q_copies):
-        copy.wait_recv()
-        part = part + q_recv[d]
-    s_send[...] = part
-    s_copies = [
-        remote(s_send, s_recv.at[e], s_sems, e, {"section": lax.rem(sec + e, ns)})
-        for e in range(1, ns)
-    ]
 
     bk_copies = []
     for d in range(n):
@@ -232,9 +235,9 @@
         if flag:
             decays = jnp.where(jnp.logical_and(row >= start, row < start + count), flag, decays)
 
-    for e, copy in zip(range(1, ns), s_copies):
-        copy.wait_recv()
-        part = part + s_recv[e]
+    arrived = q_recv.at[pl.ds(1, n * ns - 1)]
+    pltpu.make_async_copy(arrived, arrived, q_sems.at[1]).wait()
+    part = part + jnp.sum(q_recv[1:], axis=0)
     factor = clip_factor(part, numel)
     fresh, _, _ = adam_master(mean_rows[...], old_rows[0], old_rows[1], old_rows[2], decays, factor)
     w_send[...] = fresh.astype(bf16)
@@ -271,8 +274,9 @@
     for copy in stores:
         copy.start()
 
-    for copy in pair_copies + g_copies + st_copies + q_copies + s_copies + bk_copies:
+    for copy in pair_copies + g_copies + st_copies + bk_copies:
         copy.wait_send()
+    pltpu.make_async_copy(arrived, arrived, q_sems.at[0]).wait()
 
     for e in range(1, chips):
         there = w_out.at[:, cols(same_core(me, chips - e))]
@@ -338,12 +342,10 @@
             pltpu.VMEM((rows, cw), bf16),
             pltpu.VMEM((n // 2, rows, cw), bf16),
             pltpu.VMEM((slot_rows, 128), f32),
-            pltpu.VMEM((n, slot_rows, 128), f32),
-            pltpu.VMEM((slot_rows, 128), f32),
-            pltpu.VMEM((ns, slot_rows, 128), f32),
+            pltpu.VMEM((n * ns, slot_rows, 128), f32),
             pltpu.SemaphoreType.DMA((5,)),
             pltpu.SemaphoreType.DMA((n // 2,)),
-            sems(n // 2), sems(n // 2), sems(n), sems(n), sems(n), sems(n), sems(ns),
+            sems(n // 2), sems(n // 2), sems(n), sems(n), sems(n), pltpu.SemaphoreType.DMA((2,)),
             sems(n // 2), sems(n // 2),
         ],
         compiler_params=pltpu.CompilerParams(

time: 26.8 us -> 28.7 us (1.071)
  Pallas kernels: 26 us -> 27.9 us
    pallas_call x1, Pallas kernels: 23.9 us -> 25.7 us  [local(): pl.pallas_call(functools.partial(exchange, n, ns, layout, numel), out_sha...]
where the time goes in v7:
time: 28.7 us; the launch traced here: 28.6 us
  Pallas kernels  27.9 us (97%)
  between operations  0.64 us (2%)
    pallas_call x1, Pallas kernels, local(): pl.pallas_call(functools.partial(exchange, n, ns, layout, numel), out_sha...  25.7 us
    pallas_call x1, Pallas kernels, local(): pl.pallas_call(hand_out, out_shape=(jax.ShapeDtypeStruct((1, rows, width)...  2.17 us

profile of v7, /device:TPU:0, one launch (start us, length us, event | category | flops | bytes accessed | tf_op | source)
XLA Modules:
  0.0 28.6 jit_solution(18204066267733441973)
XLA Ops:
  0.6 25.7 %exchange.1 = (bf16[20,8192]{1,0:T(8,128)(2,1)}, f32[1,1,8,8192]{3,2,1,0:T(8,128)}, f32[1,1,8,8192]{3,2,1,0:T(8,128)}, f32[1,1,8,8192]{3,2,1,0:T(8,128)}, f32[1,1,8,8192]{3,2,1,0:T(8,128)}) custom-call(bf16[1,1,20,8192]{3,2,1,0:T(8,128)(2,1)} %grads.1, s32[1,6]{1,0:T(1,128)} %owners_hbm.1, f32[1,1,8,8192]{3,2,1,0:T(8,128)} %master.1, ...), custom_call_target="tpu_custom_call" | custom-call | tf_op jit(solution)/shard_map/exchange/pallas_call | solution.py:326
  26.4 2.2 %hand_out.1 = (bf16[1,20,8192]{2,1,0:T(8,128)(2,1)}, f32[1,1,8,8192]{3,2,1,0:T(8,128)}, f32[1,1,8,8192]{3,2,1,0:T(8,128)}, f32[1,1,8,8192]{3,2,1,0:T(8,128)}, f32[1,1,8,8192]{3,2,1,0:T(8,128)}) custom-call(bf16[20,8192]{1,0:T(8,128)(2,1)} %get-tuple-element.10.refs_0_, f32[1,1,8,8192]{3,2,1,0:T(8,128)} %get-tuple-element.11.refs_1_, ...), custom_call_target="tpu_custom_call" | custom-call | tf_op jit(solution)/shard_map/hand_out/pallas_call | solution.py:356
